TPU v7x, 32 devices: a whole 2x2x4 slice. The times are simulated.
32 devices in a mesh: circ: 8 (over z, y), radax: 4 (over x, core).
Axes of the slice: x: 2, y: 2, z: 4, core: 2. Of those that a mesh axis runs over, the one named last changes fastest.
Arguments:
- objective_grad: float32 [64, 64, 6, 256], P('circ', 'radax'), may hold values from -6 to 6
- adjoint_start: float32 [64, 64, 6, 256], P('circ', 'radax'), may hold values from -6 to 6
- jac_off: bfloat16 [6, 6, 64, 64, 6, 256], P(None, None, 'circ', 'radax'), may hold values from -0.625 to 0.625
- jac_diag: bfloat16 [6, 64, 64, 6, 256], P(None, 'circ', 'radax'), may hold values from -3 to 3, as said below
- precond: bfloat16 [6, 64, 64, 6, 256], P(None, 'circ', 'radax'), may hold values from -1 to 1
- face_cell: int32 [16384], P(('circ', 'radax')), may hold values from 0 to 32767
- face_side: int32 [16384], P(('circ', 'radax')), may hold values from 0 to 1
- design_grad: float32 [16384, 6, 128], P(('circ', 'radax')), may hold values from -0.0546875 to 0.0546875
Outputs:
- adjoint: float32 [64, 64, 6, 256], P('circ', 'radax')
- sensitivity: float32 [8, 128], P('circ', 'radax')
Inputs may be any that keep to these rules, and one draw needn't show every extreme that they name: face_cell indexes the cells of the device that holds the face. `jac_diag`: diagonal blocks: each diagonal entry between 1.5 and 3, off-diagonal entries of moderate size.
All inputs are finite; a program needn't handle non-finite values.
Results may differ from a plain program's by a relative error of at most 0.0003.
Values sent between devices are 32-bit elements; how exact they have to be, the bound alone decides.
A program may use at most 256 MiB of HBM per device.

v0:
```python
import jax
import jax.numpy as jnp
from jax import lax
from jax.sharding import PartitionSpec as P

NDV = 128
ITERS = 2


def extended(cells, sides, width, closed):
    for axis, dim in sides:
        count = lax.axis_size(axis)
        ends = count if closed else count - 1
        head = lax.slice_in_dim(cells, 0, width, axis=dim)
        tail = lax.slice_in_dim(cells, cells.shape[dim] - width, cells.shape[dim], axis=dim)
        cells = jnp.concatenate(
            [
                lax.ppermute(tail, axis, [(i, (i + 1) % count) for i in range(ends)]),
                cells,
                lax.ppermute(head, axis, [((i + 1) % count, i) for i in range(ends)]),
            ],
            axis=dim,
        )
    return cells


def passed_along(block, axis, distance):
    devices = range(lax.axis_size(axis))
    route = [((i - distance) % len(devices), i) for i in devices]
    return lax.ppermute(block, axis, route)


def block_apply(blocks, vector):
    summed = blocks[0].astype(jnp.float32) * vector[:, :, 0:1, :]
    for column in range(1, vector.shape[2]):
        summed = summed + blocks[column].astype(jnp.float32) * vector[:, :, column : column + 1, :]
    return summed


def neighbour_fields(field):
    wrapped = extended(field, (("circ", 0),), 1, True)
    stacked = extended(field, (("radax", 1),), 1, False)
    circ_lower = wrapped[:-2]
    circ_upper = wrapped[2:]
    rad_lower = stacked[:, :-2]
    rad_upper = stacked[:, 2:]
    axial_pad = jnp.pad(field, ((0, 0), (0, 0), (0, 0), (1, 1)))
    ax_lower = axial_pad[..., :-2]
    ax_upper = axial_pad[..., 2:]
    return [circ_lower, circ_upper, rad_lower, rad_upper, ax_lower, ax_upper]


def body(
    objective_grad, adjoint_start, jac_off, jac_diag, precond, face_cell, face_side, design_grad
):
    adjoint = adjoint_start
    for iteration in range(ITERS):
        beside = neighbour_fields(adjoint)
        applied = block_apply(jac_diag, adjoint)
        for direction in range(6):
            applied = applied + block_apply(jac_off[direction], beside[direction])
        residual = objective_grad - applied
        adjoint = adjoint + block_apply(precond, residual)
    cells_rad = adjoint.shape[1]
    cells_ax = adjoint.shape[3]
    theta = face_cell // (cells_rad * cells_ax)
    radial = face_cell // cells_ax % cells_rad
    axial = face_cell % cells_ax
    picked = adjoint[theta, radial, :, axial]
    contrib = jnp.einsum("fi,fid->fd", picked, design_grad, precision=lax.Precision.HIGHEST)
    side_table = (face_side[None, :] == jnp.arange(2, dtype=jnp.int32)[:, None]).astype(jnp.float32)
    partial_sens = jnp.dot(side_table, contrib, precision=lax.Precision.HIGHEST)
    blocks_count = lax.axis_size("radax")
    owned = NDV // blocks_count
    arrived = passed_along(partial_sens[1:2], "circ", 1)
    blade_sum = lax.psum(partial_sens[0:1] + arrived, "radax")
    sensitivity = lax.dynamic_slice_in_dim(blade_sum, lax.axis_index("radax") * owned, owned, 1)
    return (adjoint, sensitivity)


def solution(mesh):
    in_specs = (
        P("circ", "radax", None, None),
        P("circ", "radax", None, None),
        P(None, None, "circ", "radax", None, None),
        P(None, "circ", "radax", None, None),
        P(None, "circ", "radax", None, None),
        P(("circ", "radax")),
        P(("circ", "radax")),
        P(("circ", "radax"), None, None),
    )
    out_specs = (P("circ", "radax", None, None), P("circ", "radax"))
    return jax.shard_map(body, mesh=mesh, in_specs=in_specs, out_specs=out_specs, check_vma=False)
```

profile of v0, /device:TPU:0, one launch (start us, length us, event | category | flops | bytes accessed | tf_op | source)
XLA Modules:
  0.0 709.0 jit_solution(5463047717429949553)
XLA Ops:
  0.6 1.7 fusion.173
  2.4 3.0 collective-permute-start
  5.4 1.8 fusion.174
  7.2 1.3 collective-permute-start.3
  8.5 3.1 collective-permute-start.1
  11.6 3.4 collective-permute-start.2
  14.9 3.7 slice_bitcast_fusion.35
  18.6 2.7 fusion.172
  22.0 9.9 %copy.72 = f32[8,16,6,256]{2,3,1,0:T(8,128)} copy(f32[8,16,6,256]{3,1,2,0:T(8,128)} %param.9) | data formatting | bytes 1572864 | tf_op args[1]
  31.9 6.1 copy.66
  38.0 6.1 copy.67
  44.1 6.1 copy.68
  50.1 7.5 %copy.69 = bf16[1,8,16,6,256]{3,4,2,1,0:T(8,128)(2,1)} copy(bf16[1,8,16,6,256]{4,2,3,1,0:T(8,128)(2,1)} %get-tuple-element.57) | data formatting | bytes 786432 | tf_op jit(solution)/shard_map/slice | solution.py:36
  57.7 7.3 %copy.70 = bf16[1,8,16,6,256]{3,4,2,1,0:T(8,128)(2,1)} copy(bf16[1,8,16,6,256]{4,2,3,1,0:T(8,128)(2,1)} %get-tuple-element.61) | data formatting | bytes 786432 | tf_op jit(solution)/shard_map/slice | solution.py:36
  65.0 7.3 %copy.71 = bf16[1,8,16,6,256]{3,4,2,1,0:T(8,128)(2,1)} copy(bf16[1,8,16,6,256]{4,2,3,1,0:T(8,128)(2,1)} %get-tuple-element.60) | data formatting | bytes 786432 | tf_op jit(solution)/shard_map/slice | solution.py:36
  72.3 1.7 maximum_bitcast_fusion.4
  74.8 1.4 constant_dynamic-update-slice_fusion
  77.3 2.3 dynamic-update-slice.1
  79.5 1.4 slice_bitcast_fusion.17
  81.0 1.5 constant_dynamic-update-slice_fusion.2
  82.5 1.3 slice_bitcast_fusion.23
  83.8 1.3 slice_bitcast_fusion.29
  85.1 11.5 %fusion.69 = f32[8,16,6,256]{3,1,2,0:T(8,128)S(1)} fusion(f32[8,16,6,256]{3,1,2,0:T(8,128)S(1)} %copy-done.4, f32[8,16,256]{2,1,0:T(8,128)} %get-tuple-element.109, f32[8,16,256]{2,1,0:T(8,128)} %get-tuple-element.108, f32[8,16,256]{2,1,0:T(8,128)} %get-tuple-element.107, f32[8,16,256]{2,1,0:T(8,128)} %get-tuple-element.106, ...), kind=kLoop, calls=%fused_computation.230 | loop fusion | flops 24772608 | bytes 23592960 | tf_op jit(solution)/shard_map/sub | solution.py:62
  96.7 37.3 %fusion.25 = f32[8,16,6,256]{2,3,1,0:T(8,128)S(1)} fusion(f32[8,16,6,256]{2,3,1,0:T(8,128)} %copy.72, bf16[1,8,16,6,256]{3,4,2,1,0:T(8,128)(2,1)} %copy.71, bf16[1,8,16,6,256]{3,4,2,1,0:T(8,128)(2,1)} %copy.70, bf16[1,8,16,6,256]{3,4,2,1,0:T(8,128)(2,1)} %copy.69, bf16[1,8,16,6,256]{3,4,2,1,0:T(8,128)(2,1)} %copy.68, bf16[1,8,16,6,256]{3,4,2,1,0:T(8,128)(2,1)} %copy.67, ...), kind=kLoop, calls=%fused_computation.68 | loop fusion | flops 3538944 | bytes 4718592 | tf_op jit(solution)/shard_map/add | solution.py:63
  134.0 5.7 copy-done.1
  139.7 1.1 fusion.171
  140.8 204.0 %slice_reduce_fusion.5 = (f32[8,16,256]{2,1,0:T(8,128)S(1)}, f32[8,16,256]{2,1,0:T(8,128)}, f32[8,16,256]{2,1,0:T(8,128)}, f32[8,16,256]{2,1,0:T(8,128)}, f32[8,...) fusion(f32[8,16,6,256]{2,3,1,0:T(8,128)} %copy-done.1), kind=kLoop, calls=%fused_computation.108 | loop fusion | bytes 119799808 | tf_op jit(solution)/shard_map/slice | solution.py:34
  344.8 2.2 copy.77
  347.0 3.5 collective-permute-start.6
  350.4 4.7 fusion.170
  355.1 2.9 copy.73
  358.0 2.9 copy.75
  360.8 4.7 collective-permute-start.5
  366.5 1.3 collective-permute-start.7
  367.8 1.2 copy.78
  369.0 58.9 %fusion.45 = (f32[8,16,256]{2,1,0:T(8,128)}, f32[8,16,256]{2,1,0:T(8,128)}, f32[8,16,256]{2,1,0:T(8,128)}, f32[8,16,256]{2,1,0:T(8,128)}, f32[8,16,256]{2,1,0:T(8,128)}, /*index=5*/f32[8,16,256]{2,1,0:T(8,128)}) fusion(f32[8,1,6,256]{2,3,1,0:T(8,128)S(1)} %copy.78, f32[8,16,6,256]{2,3,1,0:T(8,128)} %copy-done.1), kind=kLoop, calls=%fused_computation.88 | loop fusion | flops 196608 | bytes 1622016 | tf_op jit(solution)/shard_map/slice | solution.py:34
  427.9 1.2 copy.80
  429.1 68.3 %fusion.35 = (f32[8,16,256]{2,1,0:T(8,128)}, f32[8,16,256]{2,1,0:T(8,128)}, f32[8,16,256]{2,1,0:T(8,128)}, f32[8,16,256]{2,1,0:T(8,128)}, f32[8,16,256]{2,1,0:T(8,128)}, /*index=5*/f32[8,16,256]{2,1,0:T(8,128)}) fusion(f32[8,1,6,256]{2,3,1,0:T(8,128)S(1)} %copy.80, f32[8,16,6,256]{2,3,1,0:T(8,128)} %copy-done.1), kind=kLoop, calls=%fused_computation.78 | loop fusion | flops 196608 | bytes 1622016 | tf_op jit(solution)/shard_map/slice | solution.py:34
  497.4 2.9 copy.74
  500.2 60.7 %fusion.13 = (f32[8,16,256]{2,1,0:T(8,128)}, f32[8,16,256]{2,1,0:T(8,128)}, f32[8,16,256]{2,1,0:T(8,128)}, f32[8,16,256]{2,1,0:T(8,128)}, f32[8,16,256]{2,1,0:T(8,128)}, /*index=5*/f32[8,16,256]{2,1,0:T(8,128)}) fusion(f32[8,16,6,256]{2,3,1,0:T(8,128)} %copy-done.1, f32[1,16,6,256]{2,3,1,0:T(8,128)} %copy.74), kind=kLoop, calls=%fused_computation.56 | loop fusion | flops 196608 | bytes 1671168 | tf_op jit(solution)/shard_map/slice | solution.py:34
  560.9 2.9 copy.76
  563.9 67.6 %fusion.3 = (f32[8,16,256]{2,1,0:T(8,128)S(1)}, f32[8,16,256]{2,1,0:T(8,128)S(1)}, f32[8,16,256]{2,1,0:T(8,128)S(1)}, f32[8,16,256]{2,1,0:T(8,128)S(1)}, f32[8,1...) fusion(f32[8,16,6,256]{2,3,1,0:T(8,128)} %copy-done.1, f32[1,16,6,256]{2,3,1,0:T(8,128)} %copy.76), kind=kLoop, calls=%fused_computation.46 | loop fusion | flops 196608 | bytes 1671168 | tf_op jit(solution)/shard_map/slice | solution.py:34
  631.5 11.4 %fusion.81 = f32[8,16,6,256]{3,1,2,0:T(8,128)S(1)} fusion(f32[8,16,6,256]{3,1,2,0:T(8,128)S(1)} %copy-done.4, f32[8,16,256]{2,1,0:T(8,128)} %get-tuple-element.45, f32[8,16,256]{2,1,0:T(8,128)} %get-tuple-element.44, f32[8,16,256]{2,1,0:T(8,128)} %get-tuple-element.43, f32[8,16,256]{2,1,0:T(8,128)} %get-tuple-element.42, ...), kind=kLoop, calls=%fused_computation.242 | loop fusion | flops 24772608 | bytes 23592960 | tf_op jit(solution)/shard_map/sub | solution.py:62
  643.0 37.8 %fusion.31 = f32[8,16,6,256]{2,3,1,0:T(8,128)} fusion(f32[8,16,6,256]{2,3,1,0:T(8,128)S(1)} %bitcast.308, bf16[1,8,16,6,256]{3,4,2,1,0:T(8,128)(2,1)} %copy.71, bf16[1,8,16,6,256]{3,4,2,1,0:T(8,128)(2,1)} %copy.70, bf16[1,8,16,6,256]{3,4,2,1,0:T(8,128)(2,1)} %copy.69, bf16[1,8,16,6,256]{3,4,2,1,0:T(8,128)(2,1)} %copy.68, ...), kind=kLoop, calls=%fused_computation.74 | loop fusion | flops 3538944 | bytes 4718592 | tf_op jit(solution)/shard_map/add | solution.py:63
  680.8 4.7 gather_fusion
  685.6 4.3 fusion.56
  690.2 10.8 %copy.81 = f32[8,16,6,256]{3,1,2,0:T(8,128)} copy(f32[8,16,6,256]{2,3,1,0:T(8,128)} %fusion.31) | data formatting | bytes 1572864
  701.0 7.3 %psum.7 = f32[1,128]{1,0:T(1,128)S(1)} all-reduce(f32[1,128]{1,0:T(1,128)S(1)} %slice_add_fusion), channel_id=1, replica_groups=mesh['circ'=8,'radax'=4] {'radax'}, use_global_device_ids=true, to_apply=%region_0.1 | all-reduce | flops 128 | bytes 1024 | tf_op jit(solution)/shard_map/psum | solution.py:76
  (62 shorter events, 4.6 us)
Async XLA Ops:
  0.6 684.9 %copy-start = (f32[512,6,128]{2,0,1:T(8,128)S(1)}, f32[512,6,128]{2,0,1:T(8,128)}, u32[]{:S(2)}) copy-start(f32[512,6,128]{2,0,1:T(8,128)} %param.15) | copy-start | bytes 4718596
  2.4 71.6 %collective-permute-start = (f32[1,16,6,256]{3,1,2,0:T(8,128)}, f32[1,16,6,256]{3,1,2,0:T(8,128)}, u32[]{:S(2)}, u32[]{:S(2)}) collective-permute-start(f32[1,16,6,256]{3,1,2,0:T(8,128)} %get-tuple-element.119), channel_id=1, source_target_pairs={{0,4},{4,8},{8,12},{12,16},{16,20},{20,24},{24,28},{28,0},{1,5},{5... | collective-permute-start | bytes 294920 | tf_op jit(solution)/shard_map/ppermute | solution.py:18
  7.2 70.1 %collective-permute-start.3 = (f32[8,1,6,256]{3,1,2,0:T(1,128)}, f32[8,1,6,256]{3,1,2,0:T(1,128)}, u32[]{:S(2)}, u32[]{:S(2)}) collective-permute-start(f32[8,1,6,256]{3,1,2,0:T(1,128)} %get-tuple-element.122), channel_id=1, source_target_pairs={{1,0},{2,1},{3,2},{5,4},{6,5},{7,6},{9,8},{10,9},{11,10},{13,12},{... | collective-permute-start | bytes 147464 | tf_op jit(solution)/shard_map/ppermute | solution.py:20
  8.5 72.5 %collective-permute-start.1 = (f32[1,16,6,256]{3,1,2,0:T(8,128)}, f32[1,16,6,256]{3,1,2,0:T(8,128)}, u32[]{:S(2)}, u32[]{:S(2)}) collective-permute-start(f32[1,16,6,256]{3,1,2,0:T(8,128)} %get-tuple-element.120), channel_id=1, source_target_pairs={{4,0},{8,4},{12,8},{16,12},{20,16},{24,20},{28,24},{0,28},{5,1},{9... | collective-permute-start | bytes 294920 | tf_op jit(solution)/shard_map/ppermute | solution.py:20
  11.6 60.7 %collective-permute-start.2 = (f32[8,1,6,256]{3,1,2,0:T(1,128)}, f32[8,1,6,256]{3,1,2,0:T(1,128)}, u32[]{:S(2)}, u32[]{:S(2)}) collective-permute-start(f32[8,1,6,256]{3,1,2,0:T(1,128)} %get-tuple-element.121), channel_id=1, source_target_pairs={{0,1},{1,2},{2,3},{4,5},{5,6},{6,7},{8,9},{9,10},{10,11},{12,13},{... | collective-permute-start | bytes 147464 | tf_op jit(solution)/shard_map/ppermute | solution.py:18
  44.1 28.2 %copy-start.2 = (f32[8,16,6,256]{3,1,2,0:T(8,128)S(1)}, f32[8,16,6,256]{3,1,2,0:T(8,128)}, u32[]{:S(2)}) copy-start(f32[8,16,6,256]{3,1,2,0:T(8,128)} %param.9) | copy-start | bytes 2359300
  50.1 34.9 %copy-start.4 = (f32[8,16,6,256]{3,1,2,0:T(8,128)S(1)}, f32[8,16,6,256]{3,1,2,0:T(8,128)}, u32[]{:S(2)}) copy-start(f32[8,16,6,256]{3,1,2,0:T(8,128)} %param.8) | copy-start | bytes 2359300
  50.1 34.9 %copy-start.14 = (f32[8,16,256]{2,1,0:T(8,128)S(1)}, f32[8,16,256]{2,1,0:T(8,128)}, u32[]{:S(2)}) copy-start(f32[8,16,256]{2,1,0:T(8,128)} %get-tuple-element.99) | copy-start | bytes 393220
  50.1 34.9 %copy-start.15 = (f32[8,16,256]{2,1,0:T(8,128)S(1)}, f32[8,16,256]{2,1,0:T(8,128)}, u32[]{:S(2)}) copy-start(f32[8,16,256]{2,1,0:T(8,128)} %get-tuple-element.100) | copy-start | bytes 393220
  76.3 1.0 copy-start.5
  134.0 5.7 copy-start.1
  347.0 20.8 %collective-permute-start.6 = (f32[8,1,6,256]{3,0,2,1:T(8,128)}, f32[8,1,6,256]{3,0,2,1:T(8,128)}, u32[]{:S(2)}, u32[]{:S(2)}) collective-permute-start(f32[8,1,6,256]{3,0,2,1:T(8,128)} %copy.77), channel_id=1, source_target_pairs={{0,1},{1,2},{2,3},{4,5},{5,6},{6,7},{8,9},{9,10},{10,11},{12,13},{... | collective-permute-start | bytes 147464 | tf_op jit(solution)/shard_map/ppermute | solution.py:18
  358.0 139.4 %collective-permute-start.4 = (f32[1,16,6,256]{3,1,2,0:T(8,128)}, f32[1,16,6,256]{3,1,2,0:T(8,128)}, u32[]{:S(2)}, u32[]{:S(2)}) collective-permute-start(f32[1,16,6,256]{3,1,2,0:T(8,128)} %copy.73), channel_id=1, source_target_pairs={{0,4},{4,8},{8,12},{12,16},{16,20},{20,24},{24,28},{28,0},{1,5},{5... | collective-permute-start | bytes 294920 | tf_op jit(solution)/shard_map/ppermute | solution.py:18
  360.8 200.1 %collective-permute-start.5 = (f32[1,16,6,256]{3,1,2,0:T(8,128)}, f32[1,16,6,256]{3,1,2,0:T(8,128)}, u32[]{:S(2)}, u32[]{:S(2)}) collective-permute-start(f32[1,16,6,256]{3,1,2,0:T(8,128)} %copy.75), channel_id=1, source_target_pairs={{4,0},{8,4},{12,8},{16,12},{20,16},{24,20},{28,24},{0,28},{5,1},{9... | collective-permute-start | bytes 294920 | tf_op jit(solution)/shard_map/ppermute | solution.py:20
  366.5 61.4 %collective-permute-start.7 = (f32[8,1,6,256]{3,0,2,1:T(8,128)}, f32[8,1,6,256]{3,0,2,1:T(8,128)}, u32[]{:S(2)}, u32[]{:S(2)}) collective-permute-start(f32[8,1,6,256]{3,0,2,1:T(8,128)} %copy.79), channel_id=1, source_target_pairs={{1,0},{2,1},{3,2},{5,4},{6,5},{7,6},{9,8},{10,9},{11,10},{13,12},{... | collective-permute-start | bytes 147464 | tf_op jit(solution)/shard_map/ppermute | solution.py:20
  500.2 131.2 %copy-start.6 = (f32[8,16,256]{2,1,0:T(8,128)S(1)}, f32[8,16,256]{2,1,0:T(8,128)}, u32[]{:S(2)}) copy-start(f32[8,16,256]{2,1,0:T(8,128)} %get-tuple-element.35) | copy-start | bytes 393220
  500.2 131.2 %copy-start.7 = (f32[8,16,256]{2,1,0:T(8,128)S(1)}, f32[8,16,256]{2,1,0:T(8,128)}, u32[]{:S(2)}) copy-start(f32[8,16,256]{2,1,0:T(8,128)} %get-tuple-element.36) | copy-start | bytes 393220
  563.8 67.6 %copy-start.3 = (bf16[6,8,16,6,256]{4,2,3,1,0:T(8,128)(2,1)S(1)}, bf16[6,8,16,6,256]{4,2,3,1,0:T(8,128)(2,1)}, u32[]{:S(2)}) copy-start(bf16[6,8,16,6,256]{4,2,3,1,0:T(8,128)(2,1)} %param.11) | copy-start | bytes 7077892
  563.8 67.7 %copy-start.8 = (f32[8,16,256]{2,1,0:T(8,128)S(1)}, f32[8,16,256]{2,1,0:T(8,128)}, u32[]{:S(2)}) copy-start(f32[8,16,256]{2,1,0:T(8,128)} %get-tuple-element.10) | copy-start | bytes 393220
  563.8 67.7 %copy-start.9 = (f32[8,16,256]{2,1,0:T(8,128)S(1)}, f32[8,16,256]{2,1,0:T(8,128)}, u32[]{:S(2)}) copy-start(f32[8,16,256]{2,1,0:T(8,128)} %get-tuple-element.11) | copy-start | bytes 393220
  563.8 67.7 %copy-start.10 = (f32[8,16,256]{2,1,0:T(8,128)S(1)}, f32[8,16,256]{2,1,0:T(8,128)}, u32[]{:S(2)}) copy-start(f32[8,16,256]{2,1,0:T(8,128)} %get-tuple-element.12) | copy-start | bytes 393220
  563.8 67.7 %copy-start.11 = (f32[8,16,256]{2,1,0:T(8,128)S(1)}, f32[8,16,256]{2,1,0:T(8,128)}, u32[]{:S(2)}) copy-start(f32[8,16,256]{2,1,0:T(8,128)} %get-tuple-element.13) | copy-start | bytes 393220
  563.8 67.7 %copy-start.12 = (f32[8,16,256]{2,1,0:T(8,128)S(1)}, f32[8,16,256]{2,1,0:T(8,128)}, u32[]{:S(2)}) copy-start(f32[8,16,256]{2,1,0:T(8,128)} %get-tuple-element.14) | copy-start | bytes 393220
  563.8 67.7 %copy-start.13 = (f32[8,16,256]{2,1,0:T(8,128)S(1)}, f32[8,16,256]{2,1,0:T(8,128)}, u32[]{:S(2)}) copy-start(f32[8,16,256]{2,1,0:T(8,128)} %get-tuple-element.15) | copy-start | bytes 393220
  563.8 79.1 %slice-start = ((s8[16777216]{0:T(1024)(128)(4,1)}), s8[4194304]{0:T(1024)(128)(4,1)S(1)}, s32[]{:S(2)}) async-start(s8[16777216]{0:T(1024)(128)(4,1)} %bitcast.307), calls=%async_computation | async-start | bytes 8388608
  563.9 79.1 %slice-start.1 = ((s8[16777216]{0:T(1024)(128)(4,1)}), s8[4194304]{0:T(1024)(128)(4,1)S(1)}, s32[]{:S(2)}) async-start(s8[16777216]{0:T(1024)(128)(4,1)} %bitcast.307), calls=%async_computation.1 | async-start | bytes 8388608
  631.5 11.5 %slice-start.2 = ((s8[16777216]{0:T(1024)(128)(4,1)}), s8[4194304]{0:T(1024)(128)(4,1)S(1)}, s32[]{:S(2)}) async-start(s8[16777216]{0:T(1024)(128)(4,1)} %bitcast.307), calls=%async_computation.2 | async-start | bytes 8388608
  631.5 11.5 %slice-start.3 = ((s8[16777216]{0:T(1024)(128)(4,1)}), s8[4194304]{0:T(1024)(128)(4,1)S(1)}, s32[]{:S(2)}) async-start(s8[16777216]{0:T(1024)(128)(4,1)} %bitcast.307), calls=%async_computation.3 | async-start | bytes 8388608
  643.0 46.9 %copy-start.16 = (s32[512]{0:T(512)S(1)}, s32[512]{0:T(512)}, u32[]{:S(2)}) copy-start(s32[512]{0:T(512)} %param.14) | copy-start | bytes 6148
  690.1 10.9 %collective-permute-start.8 = (f32[1,128]{1,0:T(1,128)S(1)}, f32[1,128]{1,0:T(1,128)S(1)}, u32[]{:S(2)}, u32[]{:S(2)}) collective-permute-start(f32[1,128]{1,0:T(1,128)S(1)} %slice.839), channel_id=1, source_target_pairs={{28,0},{0,4},{4,8},{8,12},{12,16},{16,20},{20,24},{24,28},{29,1},{... | collective-permute-start | bytes 1544 | tf_op jit(solution)/shard_map/ppermute | solution.py:30
where the time goes:
time: 718 us; the launch traced here: 709 us
  other arithmetic  356 us (50%)
  local copies, waits for them, and re-layouts  320 us (45%)
  starting transfers between devices  20.2 us (3%)
  blocking collectives  7.26 us (1%)
    slice x4, other arithmetic, block_apply(): summed = blocks[0].astype(jnp.float32) * vector[:, :, 0:1, :]  255 us
    slice x3, local copies, waits for them, and re-layouts, block_apply(): summed = blocks[0].astype(jnp.float32) * vector[:, :, 0:1, :]  213 us
    add x2, other arithmetic, body(): adjoint = adjoint + block_apply(precond, residual)  75.1 us
    slice x5, local copies, waits for them, and re-layouts, block_apply(): blocks[column].astype(jnp.float32) * vector[:, :, column:column + 1, :]  34.3 us
    unnamed x45, local copies, waits for them, and re-layouts  28.4 us
    sub x2, other arithmetic, body(): residual = objective_grad - applied  22.9 us
    slice x6, local copies, waits for them, and re-layouts, extended(): lax.slice_in_dim(cells, cells.shape[dim] - width, cells.shape[dim], axis=...  14.4 us
  transfers between devices with their start and end apart: 9, of which 0 were waited for; matrix products, arithmetic and copies ran while one was open for 40% of the time, Pallas kernels for 0%

commit v1 on v0

v1 whole, which is shorter than its diff:
```python
import functools

import jax
import jax.numpy as jnp
from jax import lax
from jax.experimental import pallas as pl
from jax.experimental.pallas import tpu as pltpu
from jax.sharding import PartitionSpec as P

F32 = jnp.float32
BF16 = jnp.bfloat16
MESH = pl.DeviceIdType.MESH
FACE_ROWS = 128


def kernel(
    circs, rads,
    obj_hbm, adj_hbm, off_hbm, diag_hbm, pre_hbm, cell_ref, side_ref, dg_hbm,
    out_hbm, sens_ref,
    first, second, final, off, diag, pre, dg, rad_out, rad_in, picks, table, face_at, face_side,
    sens_out, sens_in,
    adj_sem, plane_sem, dg_sem, out_sem, circ_send, circ_recv, rad_send, rad_recv,
    rad2_send, rad2_recv, sens_send, sens_recv,
):
    planes, fields, rows, axial = obj_hbm.shape
    faces = cell_ref.shape[1]
    circ = lax.axis_index("circ")
    rad = lax.axis_index("radax")
    circ_up = lax.rem(circ + 1, circs)
    circ_down = lax.rem(circ + circs - 1, circs)

    def plane_loads(t):
        return [
            pltpu.make_async_copy(off_hbm.at[:, :, t], off.at[:, :, t], plane_sem.at[t, 0]),
            pltpu.make_async_copy(diag_hbm.at[:, t], diag.at[:, t], plane_sem.at[t, 1]),
            pltpu.make_async_copy(pre_hbm.at[:, t], pre.at[:, t], plane_sem.at[t, 2]),
            pltpu.make_async_copy(obj_hbm.at[t], final.at[t], plane_sem.at[t, 3]),
        ]

    adj_load = pltpu.make_async_copy(adj_hbm, first.at[pl.ds(1, planes)], adj_sem)
    dg_load = pltpu.make_async_copy(dg_hbm, dg, dg_sem)
    adj_load.start()
    order1 = [(p + planes - 3) % planes for p in range(planes)]
    for t in order1:
        for load in plane_loads(t):
            load.start()
    dg_load.start()

    barrier = pltpu.get_barrier_semaphore()
    others = [lax.rem(rad + d, rads) for d in range(1, rads)]
    for other in others:
        pl.semaphore_signal(barrier, inc=1, device_id=(circ, other), device_id_type=MESH)
    for side in (circ_up, circ_down):
        for other in [rad] + others:
            pl.semaphore_signal(barrier, inc=1, device_id=(side, other), device_id_type=MESH)
    pl.semaphore_wait(barrier, 3 * rads - 1)

    def circ_copy(application, upward):
        target = (second if application else first).at[0 if upward else planes + 1]
        if application:
            source = second.at[planes if upward else 1]
        else:
            source = adj_hbm.at[planes - 1 if upward else 0]
        return pltpu.make_async_remote_copy(
            src_ref=source, dst_ref=target,
            send_sem=circ_send.at[application, int(upward)],
            recv_sem=circ_recv.at[application, int(upward)],
            device_id=(circ_up if upward else circ_down, rad), device_id_type=MESH,
        )

    def rad_copy(upward):
        place = 0 if upward else 1
        return pltpu.make_async_remote_copy(
            src_ref=rad_out.at[0, place], dst_ref=rad_in.at[0, place],
            send_sem=rad_send.at[place], recv_sem=rad_recv.at[place],
            device_id=(circ, rad + 1 if upward else rad - 1), device_id_type=MESH,
        )

    def rad_plane_copy(upward, t):
        place = 0 if upward else 1
        return pltpu.make_async_remote_copy(
            src_ref=rad_out.at[1, place, t], dst_ref=rad_in.at[1, place, t],
            send_sem=rad2_send.at[place, t], recv_sem=rad2_recv.at[place, t],
            device_id=(circ, rad + 1 if upward else rad - 1), device_id_type=MESH,
        )

    has_lower = rad > 0
    has_upper = rad < rads - 1

    circ_copy(0, True).start()
    circ_copy(0, False).start()

    adj_load.wait()

    def edge_rows(t, carry):
        for j in range(fields):
            field = first[t + 1, j]
            rad_out[0, 0, t, j : j + 1, :] = field[rows - 1 : rows, :]
            rad_out[0, 1, t, j : j + 1, :] = field[0:1, :]
        return carry

    lax.fori_loop(0, planes, edge_rows, 0)

    @pl.when(has_upper)
    def _():
        rad_copy(True).start()

    @pl.when(has_lower)
    def _():
        rad_copy(False).start()

    @pl.when(rad == 0)
    def _():
        for application in range(2):
            rad_in[application, 0] = jnp.zeros(rad_in.shape[2:], F32)

    @pl.when(rad == rads - 1)
    def _():
        for application in range(2):
            rad_in[application, 1] = jnp.zeros(rad_in.shape[2:], F32)

    cells = cell_ref[...].astype(F32)
    row_of = jnp.floor((cells + 0.5) * (1.0 / axial))
    ax_of = cells - row_of * axial
    lanes = lax.broadcasted_iota(jnp.int32, (FACE_ROWS, planes * rows), 1).astype(F32)
    for f in range(0, faces, FACE_ROWS):
        def spread(values):
            part = values[:, f : f + FACE_ROWS]
            return jnp.transpose(jnp.broadcast_to(part, (FACE_ROWS, FACE_ROWS)))

        row_rep = spread(row_of)[:, 0:1]
        hot = jnp.where(lanes == row_rep, 1.0, 0.0).astype(BF16)
        picks[f : f + FACE_ROWS, 0 : planes * rows] = hot
        picks[f : f + FACE_ROWS, planes * rows : 2 * planes * rows] = hot
        face_at[f : f + FACE_ROWS, :] = spread(ax_of)
        face_side[f : f + FACE_ROWS, :] = spread(side_ref[...].astype(F32))

    row_index = lax.broadcasted_iota(jnp.int32, (rows, axial), 0)
    ax_index = lax.broadcasted_iota(jnp.int32, (rows, axial), 1)

    def apply_plane(source, application, t):
        def rad_lower(j):
            halo = rad_in[application, 0, t, j : j + 1, :]
            return jnp.where(row_index == 0, halo, pltpu.roll(source[t + 1, j], 1, 0))

        def rad_upper(j):
            halo = rad_in[application, 1, t, j : j + 1, :]
            return jnp.where(row_index == rows - 1, halo, pltpu.roll(source[t + 1, j], rows - 1, 0))

        def ax_lower(j):
            return jnp.where(ax_index == 0, 0.0, pltpu.roll(source[t + 1, j], 1, 1))

        def ax_upper(j):
            return jnp.where(ax_index == axial - 1, 0.0, pltpu.roll(source[t + 1, j], axial - 1, 1))

        beside = [
            lambda j: source[t, j],
            lambda j: source[t + 2, j],
            rad_lower, rad_upper, ax_lower, ax_upper,
        ]
        applied = [None] * fields
        for j in range(fields):
            vector = source[t + 1, j]
            for i in range(fields):
                term = diag[j, t, i].astype(F32) * vector
                applied[i] = term if j == 0 else applied[i] + term
        for k in range(6):
            for j in range(fields):
                vector = beside[k](j)
                for i in range(fields):
                    applied[i] = applied[i] + off[k, j, t, i].astype(F32) * vector
        residual = [final[t, i] - applied[i] for i in range(fields)]
        result = []
        for i in range(fields):
            value = pre[0, t, i].astype(F32) * residual[0]
            for j in range(1, fields):
                value = value + pre[j, t, i].astype(F32) * residual[j]
            result.append(source[t + 1, i] + value)
        return result

    @pl.when(has_lower)
    def _():
        rad_copy(True).wait_recv()

    @pl.when(has_upper)
    def _():
        rad_copy(False).wait_recv()

    def first_step(step, carry):
        t = lax.rem(step + (planes - 3), planes)

        @pl.when(step == 2)
        def _():
            circ_copy(0, True).wait_recv()
            circ_copy(0, False).wait_recv()

        for load in plane_loads(t):
            load.wait()
        result = apply_plane(first, 0, t)
        for i in range(fields):
            second[t + 1, i] = result[i]
            rad_out[1, 0, t, i : i + 1, :] = result[i][rows - 1 : rows, :]
            rad_out[1, 1, t, i : i + 1, :] = result[i][0:1, :]

        @pl.when(has_upper)
        def _():
            rad_plane_copy(True, t).start()

        @pl.when(has_lower)
        def _():
            rad_plane_copy(False, t).start()

        @pl.when(t == 0)
        def _():
            circ_copy(1, False).start()

        @pl.when(t == planes - 1)
        def _():
            circ_copy(1, True).start()

        return carry

    lax.fori_loop(0, planes, first_step, 0)

    def second_step(step, carry):
        t = lax.rem(step + 1, planes)

        @pl.when(step == planes - 2)
        def _():
            circ_copy(1, True).wait_recv()
            circ_copy(1, False).wait_recv()

        @pl.when(has_lower)
        def _():
            rad_plane_copy(True, t).wait_recv()

        @pl.when(has_upper)
        def _():
            rad_plane_copy(False, t).wait_recv()

        result = apply_plane(second, 1, t)
        for i in range(fields):
            high = result[i].astype(BF16)
            final[t, i] = result[i]
            table[i, t] = high
            table[i, t + planes] = (result[i] - high.astype(F32)).astype(BF16)
        pltpu.make_async_copy(final.at[t], out_hbm.at[t], out_sem.at[t]).start()
        return carry

    lax.fori_loop(0, planes, second_step, 0)

    dg_load.wait()
    place = lax.broadcasted_iota(jnp.int32, (FACE_ROWS, axial), 1).astype(F32)

    def face_step(step, carry):
        lower, upper = carry
        part = pl.ds(pl.multiple_of(step * FACE_ROWS, FACE_ROWS), FACE_ROWS)
        hot = picks[part, :]
        at = face_at[part, :][:, 0:1]
        side = face_side[part, :]
        total = None
        for i in range(fields):
            values = table[i].reshape(2 * planes * rows, axial)
            row = jnp.dot(hot, values, preferred_element_type=F32)
            picked = jnp.sum(jnp.where(place == at, row, 0.0), axis=1, keepdims=True)
            term = picked * dg[i, part, :]
            total = term if i == 0 else total + term
        lower = lower + jnp.sum(jnp.where(side == 0.0, total, 0.0), axis=0, keepdims=True)
        upper = upper + jnp.sum(jnp.where(side == 1.0, total, 0.0), axis=0, keepdims=True)
        return lower, upper

    zero = jnp.zeros((1, dg.shape[2]), F32)
    lower, upper = lax.fori_loop(0, faces // FACE_ROWS, face_step, (zero, zero))
    sens_out[0] = jnp.broadcast_to(lower, sens_out.shape[1:])
    sens_out[1] = jnp.broadcast_to(upper, sens_out.shape[1:])

    def sens_copy(side, d):
        return pltpu.make_async_remote_copy(
            src_ref=sens_out.at[side], dst_ref=sens_in.at[side, d],
            send_sem=sens_send.at[side, d], recv_sem=sens_recv.at[side, d],
            device_id=(circ_up if side else circ, lax.rem(rad + d, rads)), device_id_type=MESH,
        )

    sends = [(1, d) for d in range(rads)] + [(0, d) for d in range(1, rads)]
    for side, d in sends:
        sens_copy(side, d).start()
    total = lower
    for side, d in sends:
        sens_copy(side, d).wait_recv()
        total = total + sens_in[side, d, 0:1, :]
    owned = sens_ref.shape[1]
    mine = total[:, 0:owned]
    for block in range(1, rads):
        mine = jnp.where(rad == block, total[:, block * owned : (block + 1) * owned], mine)
    sens_ref[...] = mine

    for side, d in sends:
        sens_copy(side, d).wait_send()
    for application in range(2):
        for upward in (True, False):
            circ_copy(application, upward).wait_send()

    @pl.when(has_upper)
    def _():
        rad_copy(True).wait_send()
        for t in range(planes):
            rad_plane_copy(True, t).wait_send()

    @pl.when(has_lower)
    def _():
        rad_copy(False).wait_send()
        for t in range(planes):
            rad_plane_copy(False, t).wait_send()

    for t in range(planes):
        pltpu.make_async_copy(final.at[t], out_hbm.at[t], out_sem.at[t]).wait()


def body(
    objective_grad, adjoint_start, jac_off, jac_diag, precond, face_cell, face_side, design_grad
):
    circs, rads = lax.axis_size("circ"), lax.axis_size("radax")
    planes, rows, fields, axial = adjoint_start.shape
    faces, _, variables = design_grad.shape
    state = (planes, fields, rows, axial)
    any_place = pl.BlockSpec(memory_space=pl.ANY)
    in_vmem = pl.BlockSpec(memory_space=pltpu.VMEM)
    dma = pltpu.SemaphoreType.DMA
    out, sens = pl.pallas_call(
        functools.partial(kernel, circs, rads),
        out_shape=(
            jax.ShapeDtypeStruct(state, F32),
            jax.ShapeDtypeStruct((1, variables // rads), F32),
        ),
        in_specs=[any_place] * 5 + [in_vmem] * 2 + [any_place],
        out_specs=(any_place, in_vmem),
        scratch_shapes=[
            pltpu.VMEM((planes + 2, fields, rows, axial), F32),
            pltpu.VMEM((planes + 2, fields, rows, axial), F32),
            pltpu.VMEM(state, F32),
            pltpu.VMEM((6, fields) + state, BF16),
            pltpu.VMEM((fields,) + state, BF16),
            pltpu.VMEM((fields,) + state, BF16),
            pltpu.VMEM((fields, faces, variables), F32),
            pltpu.VMEM((2, 2, planes, fields, axial), F32),
            pltpu.VMEM((2, 2, planes, fields, axial), F32),
            pltpu.VMEM((faces, 2 * planes * rows), BF16),
            pltpu.VMEM((fields, 2 * planes, rows, axial), BF16),
            pltpu.VMEM((faces, FACE_ROWS), F32),
            pltpu.VMEM((faces, FACE_ROWS), F32),
            pltpu.VMEM((2, 8, variables), F32),
            pltpu.VMEM((2, rads, 8, variables), F32),
            dma, dma((planes, 4)), dma, dma((planes,)),
            dma((2, 2)), dma((2, 2)), dma((2,)), dma((2,)),
            dma((2, planes)), dma((2, planes)), dma((2, rads)), dma((2, rads)),
        ],
        compiler_params=pltpu.CompilerParams(
            collective_id=0, has_side_effects=True, vmem_limit_bytes=62 * 1024 * 1024
        ),
        cost_estimate=pl.CostEstimate(
            flops=4 * 48 * fields * planes * rows * axial,
            bytes_accessed=48 * 2 * fields * planes * rows * axial,
            transcendentals=0,
        ),
    )(
        objective_grad.transpose(0, 2, 1, 3),
        adjoint_start.transpose(0, 2, 1, 3),
        jac_off.transpose(0, 1, 2, 4, 3, 5),
        jac_diag.transpose(0, 1, 3, 2, 4),
        precond.transpose(0, 1, 3, 2, 4),
        face_cell.reshape(1, faces),
        face_side.reshape(1, faces),
        design_grad.transpose(1, 0, 2),
    )
    return out.transpose(0, 2, 1, 3), sens


def solution(mesh):
    in_specs = (
        P("circ", "radax", None, None),
        P("circ", "radax", None, None),
        P(None, None, "circ", "radax", None, None),
        P(None, "circ", "radax", None, None),
        P(None, "circ", "radax", None, None),
        P(("circ", "radax")),
        P(("circ", "radax")),
        P(("circ", "radax"), None, None),
    )
    out_specs = (P("circ", "radax", None, None), P("circ", "radax"))
    return jax.shard_map(body, mesh=mesh, in_specs=in_specs, out_specs=out_specs, check_vma=False)
```

time: 718 us -> 35.2 us (0.05); the launches traced: 709 us -> 35 us
  other arithmetic: 356 us -> 0 us
  local copies, waits for them, and re-layouts: 320 us -> 3.15 us
  Pallas kernels: 0 us -> 31.2 us
  starting transfers between devices: 20.2 us -> 0 us
  blocking collectives: 7.26 us -> 0 us
    slice x17 -> x0, local copies, waits for them, and re-layouts: 265 us -> none  [the longest x3 213 us: block_apply(): summed = blocks[0].astype(jnp.float32) * vector[:, :, 0:1, :]]
    slice x4 -> x0, other arithmetic: 255 us -> none  [block_apply(): summed = blocks[0].astype(jnp.float32) * vector[:, :, 0:1, :]]
    add x3 -> x0, other arithmetic: 75.1 us -> none  [the longest x2 75.1 us: body(): adjoint = adjoint + block_apply(precond, residual)]
    pallas_call x0 -> x1, Pallas kernels: none -> 31.2 us  [body(): pl.pallas_call(functools.partial(kernel, circs, rads), out_shape=(jax.Sha...]
    unnamed x45 -> x2, local copies, waits for them, and re-layouts: 28.4 us -> 3.15 us
    sub x2 -> x0, other arithmetic: 22.9 us -> none  [body(): residual = objective_grad - applied]
    ppermute x9 -> x0, starting transfers between devices: 20.2 us -> none  [the longest x4 10.4 us: extended(): lax.ppermute(head, axis, [((i + 1) % count, i) for i in range(ends)])]
    ppermute x4 -> x0, local copies, waits for them, and re-layouts: 8.07 us -> none  [the longest x2 4.03 us: extended(): lax.ppermute(tail, axis, [(i, (i + 1) % count) for i in range(ends)])]
  transfers between devices with their start and end apart: 9 -> 0, of which waited for: 0 -> 0; matrix products, arithmetic and copies ran while one was open for 40% -> 0% of each run, Pallas kernels for 0% -> 0%
where the time goes in v1:
time: 35.2 us; the launch traced here: 35 us
  Pallas kernels  31.2 us (89%)
  local copies, waits for them, and re-layouts  3.15 us (9%)
  between operations  0.64 us (2%)
    pallas_call x1, Pallas kernels, body(): pl.pallas_call(functools.partial(kernel, circs, rads), out_shape=(jax.Sha...  31.2 us
    unnamed x2, local copies, waits for them, and re-layouts  3.15 us

profile of v1, /device:TPU:0, one launch (start us, length us, event | category | flops | bytes accessed | tf_op | source)
XLA Modules:
  0.0 35.0 jit_solution(13150227648556142344)
XLA Ops:
  0.6 31.2 %shard_map.95 = (f32[8,6,16,256]{3,2,1,0:T(8,128)}, f32[1,32]{1,0:T(1,128)}) custom-call(f32[8,6,16,256]{3,2,1,0:T(8,128)} %bitcast.13, f32[8,6,16,256]{3,2,1,0:T(8,128)} %bitcast.14, bf16[6,6,8,6,16,256]{5,4,3,2,1,0:T(8,128)(2,1)} %bitcast.9, bf16[6,8,6,16,256]{4,3,2,1,0:T(8,128)(2,1)} %bitcast.10, bf16[6,8,6,16,256]{4,3,2,1,0:T(8,128)(2,1)} %bitcast.11, ...), custom_call_target="tpu_custom_call" | custom-call | flops 37748736 | bytes 18874368 | tf_op jit(solution)/shard_map/pallas_call | solution.py:329
  31.8 2.1 %copy.12 = f32[8,16,6,256]{3,1,2,0:T(8,128)} copy(f32[8,16,6,256]{3,1,2,0:T(8,128)} %bitcast.15) | data formatting | bytes 1572864
  33.9 1.1 %copy.13 = f32[1,32]{1,0:T(1,128)} copy(f32[1,32]{1,0:T(1,128)} %get-tuple-element.9) | data formatting | bytes 256

commit v2 on v1

--- a/solution.py
+++ b/solution.py
@@ -11,13 +11,15 @@
 BF16 = jnp.bfloat16
 MESH = pl.DeviceIdType.MESH
 FACE_ROWS = 128
+FACE_STEP = 256
+GROUP = 3
 
 
 def kernel(
     circs, rads,
     obj_hbm, adj_hbm, off_hbm, diag_hbm, pre_hbm, cell_ref, side_ref, dg_hbm,
     out_hbm, sens_ref,
-    first, second, final, off, diag, pre, dg, rad_out, rad_in, picks, table, face_at, face_side,
+    first, second, final, off, diag, pre, dg, rad_out, rad_in, picks, table, face_at, face_side, shifted, residual,
     sens_out, sens_in,
     adj_sem, plane_sem, dg_sem, out_sem, circ_send, circ_recv, rad_send, rad_recv,
     rad2_send, rad2_recv, sens_send, sens_recv,
@@ -138,45 +140,51 @@
     row_index = lax.broadcasted_iota(jnp.int32, (rows, axial), 0)
     ax_index = lax.broadcasted_iota(jnp.int32, (rows, axial), 1)
 
-    def apply_plane(source, application, t):
-        def rad_lower(j):
-            halo = rad_in[application, 0, t, j : j + 1, :]
-            return jnp.where(row_index == 0, halo, pltpu.roll(source[t + 1, j], 1, 0))
-
-        def rad_upper(j):
-            halo = rad_in[application, 1, t, j : j + 1, :]
-            return jnp.where(row_index == rows - 1, halo, pltpu.roll(source[t + 1, j], rows - 1, 0))
-
-        def ax_lower(j):
-            return jnp.where(ax_index == 0, 0.0, pltpu.roll(source[t + 1, j], 1, 1))
-
-        def ax_upper(j):
-            return jnp.where(ax_index == axial - 1, 0.0, pltpu.roll(source[t + 1, j], axial - 1, 1))
-
-        beside = [
-            lambda j: source[t, j],
-            lambda j: source[t + 2, j],
-            rad_lower, rad_upper, ax_lower, ax_upper,
-        ]
-        applied = [None] * fields
+    def apply_plane(source, application, t, finish):
         for j in range(fields):
-            vector = source[t + 1, j]
-            for i in range(fields):
-                term = diag[j, t, i].astype(F32) * vector
-                applied[i] = term if j == 0 else applied[i] + term
-        for k in range(6):
+            centre = source[t + 1, j]
+            lower = rad_in[application, 0, t, j : j + 1, :]
+            upper = rad_in[application, 1, t, j : j + 1, :]
+            shifted[0, j] = jnp.where(row_index == 0, lower, pltpu.roll(centre, 1, 0))
+            shifted[1, j] = jnp.where(row_index == rows - 1, upper, pltpu.roll(centre, rows - 1, 0))
+            shifted[2, j] = jnp.where(ax_index == 0, 0.0, pltpu.roll(centre, 1, 1))
+            shifted[3, j] = jnp.where(ax_index == axial - 1, 0.0, pltpu.roll(centre, axial - 1, 1))
+
+        def applied_group(g, carry):
+            targets = [g * GROUP + i for i in range(GROUP)]
+            sums = [None] * GROUP
             for j in range(fields):
-                vector = beside[k](j)
-                for i in range(fields):
-                    applied[i] = applied[i] + off[k, j, t, i].astype(F32) * vector
-        residual = [final[t, i] - applied[i] for i in range(fields)]
-        result = []
-        for i in range(fields):
-            value = pre[0, t, i].astype(F32) * residual[0]
-            for j in range(1, fields):
-                value = value + pre[j, t, i].astype(F32) * residual[j]
-            result.append(source[t + 1, i] + value)
-        return result
+                vector = source[t + 1, j]
+                for n, i in enumerate(targets):
+                    term = diag[j, t, i].astype(F32) * vector
+                    sums[n] = term if j == 0 else sums[n] + term
+            for k in range(6):
+                for j in range(fields):
+                    if k < 2:
+                        vector = source[t + 2 * k, j]
+                    else:
+                        vector = shifted[k - 2, j]
+                    for n, i in enumerate(targets):
+                        sums[n] = sums[n] + off[k, j, t, i].astype(F32) * vector
+            for n, i in enumerate(targets):
+                residual[i] = final[t, i] - sums[n]
+            return carry
+
+        lax.fori_loop(0, fields // GROUP, applied_group, 0)
+
+        def result_group(g, carry):
+            targets = [g * GROUP + i for i in range(GROUP)]
+            sums = [None] * GROUP
+            for j in range(fields):
+                vector = residual[j]
+                for n, i in enumerate(targets):
+                    term = pre[j, t, i].astype(F32) * vector
+                    sums[n] = term if j == 0 else sums[n] + term
+            for n, i in enumerate(targets):
+                finish(i, source[t + 1, i] + sums[n])
+            return carry
+
+        lax.fori_loop(0, fields // GROUP, result_group, 0)
 
     @pl.when(has_lower)
     def _():
@@ -196,11 +204,15 @@
 
         for load in plane_loads(t):
             load.wait()
-        result = apply_plane(first, 0, t)
+
+        def keep(i, value):
+            second[t + 1, i] = value
+
+        apply_plane(first, 0, t, keep)
         for i in range(fields):
-            second[t + 1, i] = result[i]
-            rad_out[1, 0, t, i : i + 1, :] = result[i][rows - 1 : rows, :]
-            rad_out[1, 1, t, i : i + 1, :] = result[i][0:1, :]
+            value = second[t + 1, i]
+            rad_out[1, 0, t, i : i + 1, :] = value[rows - 1 : rows, :]
+            rad_out[1, 1, t, i : i + 1, :] = value[0:1, :]
 
         @pl.when(has_upper)
         def _():
@@ -238,39 +250,35 @@
         def _():
             rad_plane_copy(False, t).wait_recv()
 
-        result = apply_plane(second, 1, t)
-        for i in range(fields):
-            high = result[i].astype(BF16)
-            final[t, i] = result[i]
+        def keep(i, value):
+            high = value.astype(BF16)
+            final[t, i] = value
             table[i, t] = high
-            table[i, t + planes] = (result[i] - high.astype(F32)).astype(BF16)
+            table[i, t + planes] = (value - high.astype(F32)).astype(BF16)
+
+        apply_plane(second, 1, t, keep)
         pltpu.make_async_copy(final.at[t], out_hbm.at[t], out_sem.at[t]).start()
         return carry
 
     lax.fori_loop(0, planes, second_step, 0)
 
     dg_load.wait()
-    place = lax.broadcasted_iota(jnp.int32, (FACE_ROWS, axial), 1).astype(F32)
-
-    def face_step(step, carry):
-        lower, upper = carry
-        part = pl.ds(pl.multiple_of(step * FACE_ROWS, FACE_ROWS), FACE_ROWS)
+    place = lax.broadcasted_iota(jnp.int32, (FACE_STEP, axial), 1).astype(F32)
+    lower = upper = jnp.zeros((1, dg.shape[2]), F32)
+    for f in range(0, faces, FACE_STEP):
+        part = slice(f, f + FACE_STEP)
         hot = picks[part, :]
-        at = face_at[part, :][:, 0:1]
+        here = place == face_at[part, :][:, 0:1]
         side = face_side[part, :]
         total = None
         for i in range(fields):
             values = table[i].reshape(2 * planes * rows, axial)
             row = jnp.dot(hot, values, preferred_element_type=F32)
-            picked = jnp.sum(jnp.where(place == at, row, 0.0), axis=1, keepdims=True)
+            picked = jnp.sum(jnp.where(here, row, 0.0), axis=1, keepdims=True)
             term = picked * dg[i, part, :]
             total = term if i == 0 else total + term
         lower = lower + jnp.sum(jnp.where(side == 0.0, total, 0.0), axis=0, keepdims=True)
         upper = upper + jnp.sum(jnp.where(side == 1.0, total, 0.0), axis=0, keepdims=True)
-        return lower, upper
-
-    zero = jnp.zeros((1, dg.shape[2]), F32)
-    lower, upper = lax.fori_loop(0, faces // FACE_ROWS, face_step, (zero, zero))
     sens_out[0] = jnp.broadcast_to(lower, sens_out.shape[1:])
     sens_out[1] = jnp.broadcast_to(upper, sens_out.shape[1:])
 
@@ -314,6 +322,17 @@
 
     for t in range(planes):
         pltpu.make_async_copy(final.at[t], out_hbm.at[t], out_sem.at[t]).wait()
+
+
+def hand_over(state_ref, sens_ref, state_out, sens_out, sems):
+    copies = [
+        pltpu.make_async_copy(state_ref, state_out, sems.at[0]),
+        pltpu.make_async_copy(sens_ref, sens_out, sems.at[1]),
+    ]
+    for copy in copies:
+        copy.start()
+    for copy in copies:
+        copy.wait()
 
 
 def body(
@@ -348,6 +367,8 @@
             pltpu.VMEM((fields, 2 * planes, rows, axial), BF16),
             pltpu.VMEM((faces, FACE_ROWS), F32),
             pltpu.VMEM((faces, FACE_ROWS), F32),
+            pltpu.VMEM((4, fields, rows, axial), F32),
+            pltpu.VMEM((fields, rows, axial), F32),
             pltpu.VMEM((2, 8, variables), F32),
             pltpu.VMEM((2, rads, 8, variables), F32),
             dma, dma((planes, 4)), dma, dma((planes,)),
@@ -372,6 +393,17 @@
         face_side.reshape(1, faces),
         design_grad.transpose(1, 0, 2),
     )
+    out, sens = pl.pallas_call(
+        hand_over,
+        out_shape=(
+            jax.ShapeDtypeStruct(out.shape, F32),
+            jax.ShapeDtypeStruct(sens.shape, F32),
+        ),
+        in_specs=[any_place] * 2,
+        out_specs=(any_place, any_place),
+        scratch_shapes=[dma((2,))],
+        compiler_params=pltpu.CompilerParams(vmem_limit_bytes=62 * 1024 * 1024),
+    )(out, sens)
     return out.transpose(0, 2, 1, 3), sens
 
 

time: 35.2 us -> 59.3 us (1.68)
  Pallas kernels: 31.2 us -> 58.5 us
  local copies, waits for them, and re-layouts: 3.15 us -> 0 us
    pallas_call x0 -> x1, Pallas kernels: none -> 25 us  [body(): pl.pallas_call(hand_over, out_shape=(jax.ShapeDtypeStruct(out.shape, F32)...]
    unnamed x2 -> x0, local copies, waits for them, and re-layouts: 3.15 us -> none
    pallas_call x1, Pallas kernels: 31.2 us -> 33.5 us  [body(): pl.pallas_call(functools.partial(kernel, circs, rads), out_shape=(jax.Sha...]
where the time goes in v2:
time: 59.3 us; the launch traced here: 59.1 us
  Pallas kernels  58.5 us (99%)
  between operations  0.64 us (1%)
    pallas_call x1, Pallas kernels, body(): pl.pallas_call(functools.partial(kernel, circs, rads), out_shape=(jax.Sha...  33.5 us
    pallas_call x1, Pallas kernels, body(): pl.pallas_call(hand_over, out_shape=(jax.ShapeDtypeStruct(out.shape, F32)...  25 us

profile of v2, /device:TPU:0, one launch (start us, length us, event | category | flops | bytes accessed | tf_op | source)
XLA Modules:
  0.0 59.1 jit_solution(13510530685034901738)
XLA Ops:
  0.6 33.5 %shard_map.95 = (f32[8,6,16,256]{3,2,1,0:T(8,128)}, f32[1,32]{1,0:T(1,128)}) custom-call(f32[8,6,16,256]{3,2,1,0:T(8,128)} %bitcast.13, f32[8,6,16,256]{3,2,1,0:T(8,128)} %bitcast.14, bf16[6,6,8,6,16,256]{5,4,3,2,1,0:T(8,128)(2,1)} %bitcast.9, bf16[6,8,6,16,256]{4,3,2,1,0:T(8,128)(2,1)} %bitcast.10, bf16[6,8,6,16,256]{4,3,2,1,0:T(8,128)(2,1)} %bitcast.11, ...), custom_call_target="tpu_custom_call" | custom-call | flops 37748736 | bytes 18874368 | tf_op jit(solution)/shard_map/pallas_call | solution.py:348
  34.2 25.0 %shard_map.96 = (f32[8,6,16,256]{3,2,1,0:T(8,128)}, f32[1,32]{1,0:T(1,128)}) custom-call(f32[8,6,16,256]{3,2,1,0:T(8,128)} %get-tuple-element.6.state_ref, f32[1,32]{1,0:T(1,128)} %get-tuple-element.7.sens_ref), custom_call_target="tpu_custom_call" | custom-call | tf_op jit(solution)/shard_map/pallas_call | solution.py:396

commit v3 on v1

--- a/solution.py
+++ b/solution.py
@@ -11,6 +11,7 @@
 BF16 = jnp.bfloat16
 MESH = pl.DeviceIdType.MESH
 FACE_ROWS = 128
+LAG = 4
 
 
 def kernel(
@@ -40,7 +41,7 @@
     adj_load = pltpu.make_async_copy(adj_hbm, first.at[pl.ds(1, planes)], adj_sem)
     dg_load = pltpu.make_async_copy(dg_hbm, dg, dg_sem)
     adj_load.start()
-    order1 = [(p + planes - 3) % planes for p in range(planes)]
+    order1 = [(p + 3) % planes for p in range(planes)]
     for t in order1:
         for load in plane_loads(t):
             load.start()
@@ -57,10 +58,7 @@
 
     def circ_copy(application, upward):
         target = (second if application else first).at[0 if upward else planes + 1]
-        if application:
-            source = second.at[planes if upward else 1]
-        else:
-            source = adj_hbm.at[planes - 1 if upward else 0]
+        source = (second if application else first).at[planes if upward else 1]
         return pltpu.make_async_remote_copy(
             src_ref=source, dst_ref=target,
             send_sem=circ_send.at[application, int(upward)],
@@ -87,10 +85,9 @@
     has_lower = rad > 0
     has_upper = rad < rads - 1
 
+    adj_load.wait()
     circ_copy(0, True).start()
     circ_copy(0, False).start()
-
-    adj_load.wait()
 
     def edge_rows(t, carry):
         for j in range(fields):
@@ -186,14 +183,17 @@
     def _():
         rad_copy(False).wait_recv()
 
-    def first_step(step, carry):
-        t = lax.rem(step + (planes - 3), planes)
-
-        @pl.when(step == 2)
-        def _():
-            circ_copy(0, True).wait_recv()
-            circ_copy(0, False).wait_recv()
-
+    def circ_wait(application, t):
+        @pl.when(t == 0)
+        def _():
+            circ_copy(application, True).wait_recv()
+
+        @pl.when(t == planes - 1)
+        def _():
+            circ_copy(application, False).wait_recv()
+
+    def first_plane(t):
+        circ_wait(0, t)
         for load in plane_loads(t):
             load.wait()
         result = apply_plane(first, 0, t)
@@ -218,17 +218,8 @@
         def _():
             circ_copy(1, True).start()
 
-        return carry
-
-    lax.fori_loop(0, planes, first_step, 0)
-
-    def second_step(step, carry):
-        t = lax.rem(step + 1, planes)
-
-        @pl.when(step == planes - 2)
-        def _():
-            circ_copy(1, True).wait_recv()
-            circ_copy(1, False).wait_recv()
+    def second_plane(t):
+        circ_wait(1, t)
 
         @pl.when(has_lower)
         def _():
@@ -245,9 +236,19 @@
             table[i, t] = high
             table[i, t + planes] = (result[i] - high.astype(F32)).astype(BF16)
         pltpu.make_async_copy(final.at[t], out_hbm.at[t], out_sem.at[t]).start()
+
+    def both_step(step, carry):
+        @pl.when(step < planes)
+        def _():
+            first_plane(lax.rem(step + 3, planes))
+
+        @pl.when(step >= LAG)
+        def _():
+            second_plane(lax.rem(step - LAG + 4, planes))
+
         return carry
 
-    lax.fori_loop(0, planes, second_step, 0)
+    lax.fori_loop(0, planes + LAG, both_step, 0)
 
     dg_load.wait()
     place = lax.broadcasted_iota(jnp.int32, (FACE_ROWS, axial), 1).astype(F32)
@@ -314,6 +315,21 @@
 
     for t in range(planes):
         pltpu.make_async_copy(final.at[t], out_hbm.at[t], out_sem.at[t]).wait()
+
+
+def hand_over(state_ref, sens_ref, state_out, sens_out, state, sens, sems):
+    planes = state.shape[0]
+    places = [(state_ref.at[t], state.at[t], state_out.at[t]) for t in range(planes)]
+    places.append((sens_ref, sens, sens_out))
+    into = [pltpu.make_async_copy(a, b, sems.at[0, n]) for n, (a, b, c) in enumerate(places)]
+    onto = [pltpu.make_async_copy(b, c, sems.at[1, n]) for n, (a, b, c) in enumerate(places)]
+    for copy in into:
+        copy.start()
+    for n, copy in enumerate(into):
+        copy.wait()
+        onto[n].start()
+    for copy in onto:
+        copy.wait()
 
 
 def body(
@@ -372,6 +388,19 @@
         face_side.reshape(1, faces),
         design_grad.transpose(1, 0, 2),
     )
+    out, sens = pl.pallas_call(
+        hand_over,
+        out_shape=(
+            jax.ShapeDtypeStruct(out.shape, F32),
+            jax.ShapeDtypeStruct(sens.shape, F32),
+        ),
+        in_specs=[any_place] * 2,
+        out_specs=(any_place, any_place),
+        scratch_shapes=[
+            pltpu.VMEM(out.shape, F32), pltpu.VMEM(sens.shape, F32), dma((2, planes + 1)),
+        ],
+        compiler_params=pltpu.CompilerParams(vmem_limit_bytes=62 * 1024 * 1024),
+    )(out, sens)
     return out.transpose(0, 2, 1, 3), sens
 
 

time: 35.2 us -> 36.6 us (1.040)
  Pallas kernels: 31.2 us -> 35.8 us
  local copies, waits for them, and re-layouts: 3.15 us -> 0 us
    unnamed x2 -> x0, local copies, waits for them, and re-layouts: 3.15 us -> none
    pallas_call x1, Pallas kernels: 31.2 us -> 33.8 us  [body(): pl.pallas_call(functools.partial(kernel, circs, rads), out_shape=(jax.Sha...]
    pallas_call x0 -> x1, Pallas kernels: none -> 2.01 us  [body(): pl.pallas_call(hand_over, out_shape=(jax.ShapeDtypeStruct(out.shape, F32)...]
where the time goes in v3:
time: 36.6 us; the launch traced here: 36.4 us
  Pallas kernels  35.8 us (98%)
  between operations  0.64 us (2%)
    pallas_call x1, Pallas kernels, body(): pl.pallas_call(functools.partial(kernel, circs, rads), out_shape=(jax.Sha...  33.8 us
    pallas_call x1, Pallas kernels, body(): pl.pallas_call(hand_over, out_shape=(jax.ShapeDtypeStruct(out.shape, F32)...  2.01 us

profile of v3, /device:TPU:0, one launch (start us, length us, event | category | flops | bytes accessed | tf_op | source)
XLA Modules:
  0.0 36.4 jit_solution(2093622404144739887)
XLA Ops:
  0.6 33.8 %shard_map.95 = (f32[8,6,16,256]{3,2,1,0:T(8,128)}, f32[1,32]{1,0:T(1,128)}) custom-call(f32[8,6,16,256]{3,2,1,0:T(8,128)} %bitcast.13, f32[8,6,16,256]{3,2,1,0:T(8,128)} %bitcast.14, bf16[6,6,8,6,16,256]{5,4,3,2,1,0:T(8,128)(2,1)} %bitcast.9, bf16[6,8,6,16,256]{4,3,2,1,0:T(8,128)(2,1)} %bitcast.10, bf16[6,8,6,16,256]{4,3,2,1,0:T(8,128)(2,1)} %bitcast.11, ...), custom_call_target="tpu_custom_call" | custom-call | flops 37748736 | bytes 18874368 | tf_op jit(solution)/shard_map/pallas_call | solution.py:345
  34.4 2.0 %shard_map.96 = (f32[8,6,16,256]{3,2,1,0:T(8,128)}, f32[1,32]{1,0:T(1,128)}) custom-call(f32[8,6,16,256]{3,2,1,0:T(8,128)} %get-tuple-element.6.state_ref, f32[1,32]{1,0:T(1,128)} %get-tuple-element.7.sens_ref), custom_call_target="tpu_custom_call" | custom-call | tf_op jit(solution)/shard_map/pallas_call | solution.py:391

commit v4 on v1

--- a/solution.py
+++ b/solution.py
@@ -314,6 +314,21 @@
 
     for t in range(planes):
         pltpu.make_async_copy(final.at[t], out_hbm.at[t], out_sem.at[t]).wait()
+
+
+def hand_over(state_ref, sens_ref, state_out, sens_out, state, sens, sems):
+    planes = state.shape[0]
+    places = [(state_ref.at[t], state.at[t], state_out.at[t]) for t in range(planes)]
+    places.append((sens_ref, sens, sens_out))
+    into = [pltpu.make_async_copy(a, b, sems.at[0, n]) for n, (a, b, c) in enumerate(places)]
+    onto = [pltpu.make_async_copy(b, c, sems.at[1, n]) for n, (a, b, c) in enumerate(places)]
+    for copy in into:
+        copy.start()
+    for n, copy in enumerate(into):
+        copy.wait()
+        onto[n].start()
+    for copy in onto:
+        copy.wait()
 
 
 def body(
@@ -372,6 +387,19 @@
         face_side.reshape(1, faces),
         design_grad.transpose(1, 0, 2),
     )
+    out, sens = pl.pallas_call(
+        hand_over,
+        out_shape=(
+            jax.ShapeDtypeStruct(out.shape, F32),
+            jax.ShapeDtypeStruct(sens.shape, F32),
+        ),
+        in_specs=[any_place] * 2,
+        out_specs=(any_place, any_place),
+        scratch_shapes=[
+            pltpu.VMEM(out.shape, F32), pltpu.VMEM(sens.shape, F32), dma((2, planes + 1)),
+        ],
+        compiler_params=pltpu.CompilerParams(vmem_limit_bytes=62 * 1024 * 1024),
+    )(out, sens)
     return out.transpose(0, 2, 1, 3), sens
 
 

time: 35.2 us -> 34.1 us (0.969)
  local copies, waits for them, and re-layouts: 3.15 us -> 0 us
  Pallas kernels: 31.2 us -> 33.3 us
    unnamed x2 -> x0, local copies, waits for them, and re-layouts: 3.15 us -> none
    pallas_call x0 -> x1, Pallas kernels: none -> 2.01 us  [body(): pl.pallas_call(hand_over, out_shape=(jax.ShapeDtypeStruct(out.shape, F32)...]
where the time goes in v4:
time: 34.1 us; the launch traced here: 33.9 us
  Pallas kernels  33.3 us (98%)
  between operations  0.64 us (2%)
    pallas_call x1, Pallas kernels, body(): pl.pallas_call(functools.partial(kernel, circs, rads), out_shape=(jax.Sha...  31.2 us
    pallas_call x1, Pallas kernels, body(): pl.pallas_call(hand_over, out_shape=(jax.ShapeDtypeStruct(out.shape, F32)...  2.01 us

profile of v4, /device:TPU:0, one launch (start us, length us, event | category | flops | bytes accessed | tf_op | source)
XLA Modules:
  0.0 33.9 jit_solution(1788026054936927666)
XLA Ops:
  0.6 31.2 %shard_map.95 = (f32[8,6,16,256]{3,2,1,0:T(8,128)}, f32[1,32]{1,0:T(1,128)}) custom-call(f32[8,6,16,256]{3,2,1,0:T(8,128)} %bitcast.13, f32[8,6,16,256]{3,2,1,0:T(8,128)} %bitcast.14, bf16[6,6,8,6,16,256]{5,4,3,2,1,0:T(8,128)(2,1)} %bitcast.9, bf16[6,8,6,16,256]{4,3,2,1,0:T(8,128)(2,1)} %bitcast.10, bf16[6,8,6,16,256]{4,3,2,1,0:T(8,128)(2,1)} %bitcast.11, ...), custom_call_target="tpu_custom_call" | custom-call | flops 37748736 | bytes 18874368 | tf_op jit(solution)/shard_map/pallas_call | solution.py:344
  31.9 2.0 %shard_map.96 = (f32[8,6,16,256]{3,2,1,0:T(8,128)}, f32[1,32]{1,0:T(1,128)}) custom-call(f32[8,6,16,256]{3,2,1,0:T(8,128)} %get-tuple-element.6.state_ref, f32[1,32]{1,0:T(1,128)} %get-tuple-element.7.sens_ref), custom_call_target="tpu_custom_call" | custom-call | tf_op jit(solution)/shard_map/pallas_call | solution.py:390

commit v5 on v4

--- a/solution.py
+++ b/solution.py
@@ -17,7 +17,7 @@
     circs, rads,
     obj_hbm, adj_hbm, off_hbm, diag_hbm, pre_hbm, cell_ref, side_ref, dg_hbm,
     out_hbm, sens_ref,
-    first, second, final, off, diag, pre, dg, rad_out, rad_in, picks, table, face_at, face_side,
+    states, final, off, diag, pre, dg, rad_out, rad_in, picks, table, face_at, face_side, latest,
     sens_out, sens_in,
     adj_sem, plane_sem, dg_sem, out_sem, circ_send, circ_recv, rad_send, rad_recv,
     rad2_send, rad2_recv, sens_send, sens_recv,
@@ -37,7 +37,7 @@
             pltpu.make_async_copy(obj_hbm.at[t], final.at[t], plane_sem.at[t, 3]),
         ]
 
-    adj_load = pltpu.make_async_copy(adj_hbm, first.at[pl.ds(1, planes)], adj_sem)
+    adj_load = pltpu.make_async_copy(adj_hbm, states.at[0, pl.ds(1, planes)], adj_sem)
     dg_load = pltpu.make_async_copy(dg_hbm, dg, dg_sem)
     adj_load.start()
     order1 = [(p + planes - 3) % planes for p in range(planes)]
@@ -56,9 +56,9 @@
     pl.semaphore_wait(barrier, 3 * rads - 1)
 
     def circ_copy(application, upward):
-        target = (second if application else first).at[0 if upward else planes + 1]
+        target = states.at[application, 0 if upward else planes + 1]
         if application:
-            source = second.at[planes if upward else 1]
+            source = states.at[1, planes if upward else 1]
         else:
             source = adj_hbm.at[planes - 1 if upward else 0]
         return pltpu.make_async_remote_copy(
@@ -94,7 +94,7 @@
 
     def edge_rows(t, carry):
         for j in range(fields):
-            field = first[t + 1, j]
+            field = states[0, t + 1, j]
             rad_out[0, 0, t, j : j + 1, :] = field[rows - 1 : rows, :]
             rad_out[0, 1, t, j : j + 1, :] = field[0:1, :]
         return carry
@@ -138,29 +138,29 @@
     row_index = lax.broadcasted_iota(jnp.int32, (rows, axial), 0)
     ax_index = lax.broadcasted_iota(jnp.int32, (rows, axial), 1)
 
-    def apply_plane(source, application, t):
+    def apply_plane(application, t):
         def rad_lower(j):
             halo = rad_in[application, 0, t, j : j + 1, :]
-            return jnp.where(row_index == 0, halo, pltpu.roll(source[t + 1, j], 1, 0))
+            return jnp.where(row_index == 0, halo, pltpu.roll(states[application, t + 1, j], 1, 0))
 
         def rad_upper(j):
             halo = rad_in[application, 1, t, j : j + 1, :]
-            return jnp.where(row_index == rows - 1, halo, pltpu.roll(source[t + 1, j], rows - 1, 0))
+            return jnp.where(row_index == rows - 1, halo, pltpu.roll(states[application, t + 1, j], rows - 1, 0))
 
         def ax_lower(j):
-            return jnp.where(ax_index == 0, 0.0, pltpu.roll(source[t + 1, j], 1, 1))
+            return jnp.where(ax_index == 0, 0.0, pltpu.roll(states[application, t + 1, j], 1, 1))
 
         def ax_upper(j):
-            return jnp.where(ax_index == axial - 1, 0.0, pltpu.roll(source[t + 1, j], axial - 1, 1))
+            return jnp.where(ax_index == axial - 1, 0.0, pltpu.roll(states[application, t + 1, j], axial - 1, 1))
 
         beside = [
-            lambda j: source[t, j],
-            lambda j: source[t + 2, j],
+            lambda j: states[application, t, j],
+            lambda j: states[application, t + 2, j],
             rad_lower, rad_upper, ax_lower, ax_upper,
         ]
         applied = [None] * fields
         for j in range(fields):
-            vector = source[t + 1, j]
+            vector = states[application, t + 1, j]
             for i in range(fields):
                 term = diag[j, t, i].astype(F32) * vector
                 applied[i] = term if j == 0 else applied[i] + term
@@ -175,7 +175,7 @@
             value = pre[0, t, i].astype(F32) * residual[0]
             for j in range(1, fields):
                 value = value + pre[j, t, i].astype(F32) * residual[j]
-            result.append(source[t + 1, i] + value)
+            result.append(states[application, t + 1, i] + value)
         return result
 
     @pl.when(has_lower)
@@ -186,68 +186,72 @@
     def _():
         rad_copy(False).wait_recv()
 
-    def first_step(step, carry):
-        t = lax.rem(step + (planes - 3), planes)
-
-        @pl.when(step == 2)
+    def plane_step(step, carry):
+        application = step // planes
+        t = lax.rem(step + (planes - 3) + 4 * application, planes)
+
+        for before, place in ((0, 2), (1, 2 * planes - 2)):
+            @pl.when(step == place)
+            def _():
+                circ_copy(before, True).wait_recv()
+                circ_copy(before, False).wait_recv()
+
+        @pl.when(application == 0)
         def _():
-            circ_copy(0, True).wait_recv()
-            circ_copy(0, False).wait_recv()
-
-        for load in plane_loads(t):
-            load.wait()
-        result = apply_plane(first, 0, t)
+            for load in plane_loads(t):
+                load.wait()
+
+        @pl.when(application == 1)
+        def _():
+            @pl.when(has_lower)
+            def _():
+                rad_plane_copy(True, t).wait_recv()
+
+            @pl.when(has_upper)
+            def _():
+                rad_plane_copy(False, t).wait_recv()
+
+        result = apply_plane(application, t)
         for i in range(fields):
-            second[t + 1, i] = result[i]
-            rad_out[1, 0, t, i : i + 1, :] = result[i][rows - 1 : rows, :]
-            rad_out[1, 1, t, i : i + 1, :] = result[i][0:1, :]
-
-        @pl.when(has_upper)
+            latest[i] = result[i]
+
+        @pl.when(application == 0)
         def _():
-            rad_plane_copy(True, t).start()
-
-        @pl.when(has_lower)
+            for i in range(fields):
+                value = latest[i]
+                states[1, t + 1, i] = value
+                rad_out[1, 0, t, i : i + 1, :] = value[rows - 1 : rows, :]
+                rad_out[1, 1, t, i : i + 1, :] = value[0:1, :]
+
+            @pl.when(has_upper)
+            def _():
+                rad_plane_copy(True, t).start()
+
+            @pl.when(has_lower)
+            def _():
+                rad_plane_copy(False, t).start()
+
+            @pl.when(t == 0)
+            def _():
+                circ_copy(1, False).start()
+
+            @pl.when(t == planes - 1)
+            def _():
+                circ_copy(1, True).start()
+
+        @pl.when(application == 1)
         def _():
-            rad_plane_copy(False, t).start()
-
-        @pl.when(t == 0)
-        def _():
-            circ_copy(1, False).start()
-
-        @pl.when(t == planes - 1)
-        def _():
-            circ_copy(1, True).start()
+            for i in range(fields):
+                value = latest[i]
+                high = value.astype(BF16)
+                final[t, i] = value
+                table[i, t] = high
+                table[i, t + planes] = (value - high.astype(F32)).astype(BF16)
+            pltpu.make_async_copy(final.at[t], out_hbm.at[t], out_sem.at[t]).start()
 
         return carry
 
-    lax.fori_loop(0, planes, first_step, 0)
-
-    def second_step(step, carry):
-        t = lax.rem(step + 1, planes)
-
-        @pl.when(step == planes - 2)
-        def _():
-            circ_copy(1, True).wait_recv()
-            circ_copy(1, False).wait_recv()
-
-        @pl.when(has_lower)
-        def _():
-            rad_plane_copy(True, t).wait_recv()
-
-        @pl.when(has_upper)
-        def _():
-            rad_plane_copy(False, t).wait_recv()
-
-        result = apply_plane(second, 1, t)
-        for i in range(fields):
-            high = result[i].astype(BF16)
-            final[t, i] = result[i]
-            table[i, t] = high
-            table[i, t + planes] = (result[i] - high.astype(F32)).astype(BF16)
-        pltpu.make_async_copy(final.at[t], out_hbm.at[t], out_sem.at[t]).start()
-        return carry
-
-    lax.fori_loop(0, planes, second_step, 0)
+    lax.fori_loop(0, 2 * planes, plane_step, 0)
 
     dg_load.wait()
     place = lax.broadcasted_iota(jnp.int32, (FACE_ROWS, axial), 1).astype(F32)
@@ -350,8 +354,7 @@
         in_specs=[any_place] * 5 + [in_vmem] * 2 + [any_place],
         out_specs=(any_place, in_vmem),
         scratch_shapes=[
-            pltpu.VMEM((planes + 2, fields, rows, axial), F32),
-            pltpu.VMEM((planes + 2, fields, rows, axial), F32),
+            pltpu.VMEM((2, planes + 2, fields, rows, axial), F32),
             pltpu.VMEM(state, F32),
             pltpu.VMEM((6, fields) + state, BF16),
             pltpu.VMEM((fields,) + state, BF16),
@@ -363,6 +366,7 @@
             pltpu.VMEM((fields, 2 * planes, rows, axial), BF16),
             pltpu.VMEM((faces, FACE_ROWS), F32),
             pltpu.VMEM((faces, FACE_ROWS), F32),
+            pltpu.VMEM((fields, rows, axial), F32),
             pltpu.VMEM((2, 8, variables), F32),
             pltpu.VMEM((2, rads, 8, variables), F32),
             dma, dma((planes, 4)), dma, dma((planes,)),

time: 34.1 us -> 34.3 us (level)
  no operation moved by 1% of the time
where the time goes in v5:
time: 34.3 us; the launch traced here: 34.1 us
  Pallas kernels  33.5 us (98%)
  between operations  0.64 us (2%)
    pallas_call x1, Pallas kernels, body(): pl.pallas_call(functools.partial(kernel, circs, rads), out_shape=(jax.Sha...  31.4 us
    pallas_call x1, Pallas kernels, body(): pl.pallas_call(hand_over, out_shape=(jax.ShapeDtypeStruct(out.shape, F32)...  2.01 us

profile of v5, /device:TPU:0, one launch (start us, length us, event | category | flops | bytes accessed | tf_op | source)
XLA Modules:
  0.0 34.1 jit_solution(15515240109182422712)
XLA Ops:
  0.6 31.4 %shard_map.95 = (f32[8,6,16,256]{3,2,1,0:T(8,128)}, f32[1,32]{1,0:T(1,128)}) custom-call(f32[8,6,16,256]{3,2,1,0:T(8,128)} %bitcast.13, f32[8,6,16,256]{3,2,1,0:T(8,128)} %bitcast.14, bf16[6,6,8,6,16,256]{5,4,3,2,1,0:T(8,128)(2,1)} %bitcast.9, bf16[6,8,6,16,256]{4,3,2,1,0:T(8,128)(2,1)} %bitcast.10, bf16[6,8,6,16,256]{4,3,2,1,0:T(8,128)(2,1)} %bitcast.11, ...), custom_call_target="tpu_custom_call" | custom-call | flops 37748736 | bytes 18874368 | tf_op jit(solution)/shard_map/pallas_call | solution.py:348
  32.1 2.0 %shard_map.96 = (f32[8,6,16,256]{3,2,1,0:T(8,128)}, f32[1,32]{1,0:T(1,128)}) custom-call(f32[8,6,16,256]{3,2,1,0:T(8,128)} %get-tuple-element.6.state_ref, f32[1,32]{1,0:T(1,128)} %get-tuple-element.7.sens_ref), custom_call_target="tpu_custom_call" | custom-call | tf_op jit(solution)/shard_map/pallas_call | solution.py:394
